TPU v7x, 128 devices: a whole 4x4x4 slice. The times are simulated.
128 devices in a mesh: lb: 16 (over z_lo, y, core), rb: 8 (over x, z_hi).
Axes of the slice: x: 4, y: 4, z: 4 (z_hi: 2, z_lo: 2; z = z_hi * 2 + z_lo), core: 2. Of those that a mesh axis runs over, the one named last changes fastest.
Arguments:
- wavefunction: bfloat16 [3072, 4, 3072], P('lb', None, 'rb'), may hold values from -6 to 6
- left_environment: bfloat16 [8, 2048, 3072], P(None, 'lb'), may hold values from -0.109375 to 0.109375
- operator_left: float32 [8, 8, 2, 2], replicated, may hold values from -1.5 to 1.5
- operator_right: float32 [8, 8, 2, 2], replicated, may hold values from -1.5 to 1.5
- right_environment: bfloat16 [8, 3072, 3072], P(None, 'rb', 'lb'), may hold values from -0.0546875 to 0.0546875
- row_sector: int32 [16], replicated, may hold values from 0 to 7, never falling along the last dimension, each value on 1 to 4 neighbouring positions
Outputs:
- applied_state: bfloat16 [2048, 4, 3072], P('lb', None, 'rb')
- density: float32 [2048, 2048], P('lb', 'rb')
Inputs may be any that keep to these rules, and one draw needn't show every extreme that they name: `row_sector`: entry t is the sector of output rows t * 128 to (t + 1) * 128 - 1. Entries never fall along t; each sector holds 1 to 4 tiles, and one holds exactly 4.
All inputs are finite; a program needn't handle non-finite values.
Results may differ from a plain program's by a relative error of at most 0.013.
Values may be sent and summed in bfloat16 or wider, within the bound.
A program may use at most 128 MiB of HBM per device.

v0:
```python
import math
import jax
import jax.numpy as jnp
from jax import lax
from jax.sharding import Mesh
from jax.sharding import PartitionSpec as P

BOND_WIDTH = 3072
SECTOR_TILES = 4
RB = ("rb_0", "rb_1")


def shifted(value, axis, by):
    devices = lax.axis_size(axis)
    pairs = [(i, i + by) for i in range(devices) if 0 <= i + by < devices]
    return lax.ppermute(value, axis, pairs)


def summed_rows(value, axes, dim):
    for axis in axes:
        value = lax.psum_scatter(value, axis, scatter_dimension=dim, tiled=True)
    return value


def split_up(value, dim, devices):
    before, after = (value.shape[:dim], value.shape[dim + 1 :])
    return jnp.moveaxis(value.reshape(*before, devices, -1, *after), dim, 0)


def sent_and_summed(value, axis, dim):
    parts = split_up(value, dim, lax.axis_size(axis))
    arrived = lax.all_to_all(parts, axis, split_axis=0, concat_axis=0, tiled=True)
    return arrived.astype(jnp.float32).sum(axis=0)


def combine_operators(operator_left, operator_right):
    channels = operator_left.shape[0]
    joined = jnp.einsum(
        "aups,uvqt->avpqst", operator_left, operator_right, precision=lax.Precision.HIGHEST
    )
    return joined.reshape(channels, channels, 4, 4)


def label_at(labels, position):
    matches = jnp.arange(labels.shape[0], dtype=jnp.int32) == position
    return (jnp.sum(jnp.where(matches, labels, 0)), jnp.any(matches))


def tile_gram(left_tile, right_tile):
    return lax.dot_general(
        left_tile, right_tile, (((1,), (1,)), ((), ())), preferred_element_type=jnp.float32
    )


def fetch_tile(own_tile, offset):
    return shifted(own_tile, "lb", -offset)


def shards(
    wavefunction, left_environment, operator_left, operator_right, right_environment, row_sector
):
    channels, row_count, full_bond = left_environment.shape
    local_right = wavefunction.shape[2]
    left_matrix = left_environment.reshape(channels * row_count, full_bond)
    rows_piece = lax.all_gather(wavefunction, "lb", axis=0, tiled=True)
    flat_piece = rows_piece.reshape(rows_piece.shape[0], 4 * local_right)
    left_part = jnp.dot(left_matrix, flat_piece, preferred_element_type=jnp.float32)
    left_part = left_part.reshape(channels, row_count, 4, local_right)
    combined = combine_operators(operator_left, operator_right)
    mixed_part = jnp.einsum(
        "avyx,alxr->lyvr", combined, left_part, precision=lax.Precision.HIGHEST
    ).astype(jnp.bfloat16)
    mixed_matrix = mixed_part.reshape(row_count * 4, channels * local_right)
    columns_piece = lax.all_gather(right_environment, "lb", axis=2, tiled=True)
    flat_piece = columns_piece.reshape(channels * local_right, columns_piece.shape[2])
    partial_value = jnp.dot(mixed_matrix, flat_piece, preferred_element_type=jnp.float32)
    summed = summed_rows(partial_value.astype(jnp.bfloat16), RB, 1).astype(jnp.float32)
    applied = summed.astype(jnp.bfloat16).reshape(row_count, 4, summed.shape[1])
    own_tile = applied.reshape(row_count, 4 * summed.shape[1])
    own_index = lax.axis_index("lb")
    tile_count = lax.axis_size("lb")
    reach_tiles = SECTOR_TILES - 1
    own_label = label_at(row_sector, own_index)[0]
    buffer = jnp.zeros((row_count, (tile_count + 2 * reach_tiles) * row_count), jnp.float32)

    def place_block(buffer, gram_block, offset):
        mate_index = own_index + offset
        mate_label, inside = label_at(row_sector, mate_index)
        keep_block = jnp.logical_and(inside, mate_label == own_label)
        gram_block = jnp.where(keep_block, gram_block, jnp.float32(0.0))
        column_start = (mate_index + reach_tiles) * row_count
        return lax.dynamic_update_slice(buffer, gram_block, (jnp.int32(0), column_start))

    buffer = place_block(buffer, tile_gram(own_tile, own_tile), 0)
    for distance in range(1, SECTOR_TILES):
        gram_block = tile_gram(own_tile, fetch_tile(own_tile, distance))
        buffer = place_block(buffer, gram_block, distance)
        returned = shifted(gram_block.astype(jnp.bfloat16), "lb", distance).astype(gram_block.dtype)
        buffer = place_block(buffer, returned.T, -distance)
    full_rows = buffer[:, reach_tiles * row_count : (reach_tiles + tile_count) * row_count]
    density = sent_and_summed(full_rows.astype(jnp.bfloat16), RB, 1) * (
        1.0 / math.sqrt(4.0 * BOND_WIDTH)
    )
    return (applied, density)


def solution(mesh):
    torus = Mesh(mesh.devices.reshape(mesh.shape["lb"], 4, 2), ("lb", "rb_0", "rb_1"))
    in_specs = (P("lb", None, RB), P(None, "lb", None), P(), P(), P(None, RB, "lb"), P())
    out_specs = (P("lb", None, RB), P("lb", RB))
    return jax.shard_map(
        shards, mesh=torus, in_specs=in_specs, out_specs=out_specs, check_vma=False
    )
```

profile of v0, /device:TPU:1, one launch (start us, length us, event | category | flops | bytes accessed | tf_op | source)
XLA Modules:
  0.0 340.6 jit_solution(16183151076118569877)
XLA Ops:
  7.2 0.7 all-gather.3.cloned.1.call-update
  8.0 3.0 copy.27
  11.0 1.1 convolution_bitcast_fusion
  12.2 0.7 copy.25
  12.9 57.6 %all-gather.3.cloned.1.call-done = bf16[3072,4,384]{2,1,0:T(4,128)(2,1)} async-done(((bf16[192,4,384]{2,1,0:T(4,128)(2,1)}), bf16[3072,4,384]{2,1,0:T(4,128)(2,1)}) %all-gather.3.cloned.1.call-update) | async-done | bytes 9437200 | tf_op jit(solution)/shard_map/all_gather | solution.py:65
  70.5 15.5 %copy.41 = bf16[3072,4,384]{0,2,1:T(8,128)(2,1)} copy(bf16[3072,4,384]{2,1,0:T(4,128)(2,1)} %all-gather.3.cloned.1.call-done) | data formatting | bytes 18874368 | tf_op jit(solution)/shard_map/reshape | solution.py:66
  85.9 15.1 %fusion = f32[8,128,4,384]{3,0,2,1:T(8,128)S(1)} fusion(bf16[3072,4,384]{0,2,1:T(8,128)(2,1)} %copy.41, bf16[8,128,3072,1]{2,1,0,3:T(8,128)(2,1)} %bitcast.62), kind=kOutput, calls=%fused_computation | convolution fusion | flops 9663676416 | bytes 22020096 | tf_op jit(solution)/shard_map/dot_general | solution.py:67
  101.1 5.7 %bitcast_convert_fusion = bf16[128,384,8,4]{1,2,3,0:T(8,128)(2,1)S(1)} fusion(f32[8,8,4,4,1]{1,0,3,2,4:T(8,128)S(1)} %bitcast.60, f32[8,128,4,384]{3,0,2,1:T(8,128)S(1)} %fusion), kind=kOutput, calls=%fused_computation.4 | convolution fusion | flops 605552640 | bytes 9441280 | tf_op jit(solution)/shard_map/avyx,alxr->lyvr/dot_general | solution.py:70
  106.8 0.7 copy.49
  107.5 67.1 %all-gather.5.cloned.1.call-done = bf16[8,384,3072]{1,0,2:T(8,128)(2,1)} async-done(((bf16[8,384,192]{1,0,2:T(8,128)(2,1)}), bf16[8,384,3072]{1,0,2:T(8,128)(2,1)}) %all-gather.5.cloned.1.call-update) | async-done | bytes 18874384 | tf_op jit(solution)/shard_map/all_gather | solution.py:74
  174.6 24.0 %copy.28 = bf16[8,384,3072]{2,1,0:T(8,128)(2,1)} copy(bf16[8,384,3072]{1,0,2:T(8,128)(2,1)} %all-gather.5.cloned.1.call-done) | data formatting | bytes 37748736 | tf_op jit(solution)/shard_map/all_gather | solution.py:74
  198.6 15.1 %convolution_convert_fusion = bf16[512,3072]{1,0:T(8,128)(2,1)} fusion(bf16[512,3072]{1,0:T(8,128)(2,1)S(1)} %bitcast.57, bf16[3072,3072]{1,0:T(8,128)(2,1)} %bitcast.55), kind=kOutput, calls=%fused_computation.6 | convolution fusion | flops 9665249280 | bytes 25165824 | tf_op jit(solution)/shard_map/dot_general | solution.py:76
  213.8 38.6 %reduce-scatter.5.cloned.1.call-done = bf16[512,768]{1,0:T(8,128)(2,1)} async-done(((bf16[512,3072]{1,0:T(8,128)(2,1)}), bf16[512,768]{1,0:T(8,128)(2,1)}) %reduce-scatter.5.cloned.1.call-update) | async-done | bytes 786448 | tf_op jit(solution)/shard_map/reduce_scatter | solution.py:21
  252.4 2.3 copy.47
  254.8 21.5 %reduce-scatter.7.cloned.1.call-done = bf16[384,512]{1,0:T(8,128)(2,1)} async-done(((bf16[768,512]{1,0:T(8,128)(2,1)}), bf16[384,512]{1,0:T(8,128)(2,1)}) %reduce-scatter.7.cloned.1.call-update) | async-done | bytes 393232
  276.2 1.2 copy.48
  277.7 2.6 collective-permute-start
  281.5 0.7 fusion.16
  284.2 1.3 collective-permute-start.2
  285.6 0.9 fusion.7
  287.1 3.3 collective-permute-start.1
  290.5 0.6 compare_reduce_fusion.4
  295.5 1.3 collective-permute-start.4
  297.4 4.2 %collective-permute-start.3 = (bf16[128,128]{0,1:T(8,128)(2,1)S(1)}, bf16[128,128]{0,1:T(8,128)(2,1)S(1)}, u32[]{:S(2)}, u32[]{:S(2)}) collective-permute-start(bf16[128,128]{0,1:T(8,128)(2,1)S(1)} %get-tuple-element.14), channel_id=1, source_target_pairs={{0,16},{8,24},{16,32},{24,40},{32,48},{40,56},{48,64},{56,72},{64,... | collective-permute-start | bytes 98312 | tf_op jit(solution)/shard_map/ppermute | solution.py:16
  301.6 0.6 compare_reduce_fusion.2
  306.9 8.5 %collective-permute-start.5 = (bf16[128,128]{0,1:T(8,128)(2,1)S(1)}, bf16[128,128]{0,1:T(8,128)(2,1)S(1)}, u32[]{:S(2)}, u32[]{:S(2)}) collective-permute-start(bf16[128,128]{0,1:T(8,128)(2,1)S(1)} %get-tuple-element.16), channel_id=1, source_target_pairs={{0,24},{8,32},{16,40},{24,48},{32,56},{40,64},{48,72},{56,80},{64,... | collective-permute-start | bytes 98312 | tf_op jit(solution)/shard_map/ppermute | solution.py:16
  315.4 0.6 compare_reduce_fusion
  318.2 0.8 slice.7
  319.0 4.0 %all-to-all-start = ((bf16[8,128,256]{1,2,0:T(8,128)(2,1)}), bf16[8,128,256]{1,2,0:T(8,128)(2,1)S(1)}, u32[]{:S(2)}, u32[]{:S(2)}) async-start(bf16[8,128,256]{1,2,0:T(8,128)(2,1)} %bitcast.20), calls=%async_computation.1 | async-start | bytes 1048576 | tf_op jit(solution)/shard_map/all_to_all | solution.py:32
  323.0 0.8 reshape.31
  323.8 9.3 %all-to-all-done = bf16[8,128,256]{1,2,0:T(8,128)(2,1)S(1)} async-done(((bf16[8,128,256]{1,2,0:T(8,128)(2,1)}), bf16[8,128,256]{1,2,0:T(8,128)(2,1)S(1)}, u32[]{:S(2)}, u32[]{:S(2)}) %all-to-all-start) | async-done | bytes 524320 | tf_op jit(solution)/shard_map/all_to_all | solution.py:32
  333.3 0.8 copy.32
  (41 shorter events, 4.9 us)
Async XLA Ops:
  7.2 3.9 %copy-start = (f32[8,8,2,2]{1,3,2,0:T(2,128)S(1)}, f32[8,8,2,2]{1,3,2,0:T(2,128)}, u32[]{:S(2)}) copy-start(f32[8,8,2,2]{1,3,2,0:T(2,128)} %param.8) | copy-start | bytes 3076
  7.2 63.3 %all-gather.3.cloned.1.call-start = ((), (), s32[]{:S(2)}) async-start(), calls=%async_computation.3 | async-start | bytes 10027008 | tf_op jit(solution)/shard_map/all_gather | solution.py:65
  7.9 166.7 %all-gather.5.cloned.1.call-start = ((), (), s32[]{:S(2)}) async-start(), calls=%async_computation.4 | async-start | bytes 20054016 | tf_op jit(solution)/shard_map/all_gather | solution.py:74
  11.0 241.5 %reduce-scatter.5.cloned.1.call-start = ((), (), s32[]{:S(2)}) async-start(), calls=%async_computation.5 | async-start | bytes 3932160 | tf_op jit(solution)/shard_map/reduce_scatter | solution.py:21
  85.9 15.2 %copy-start.2 = (f32[8,8,2,2,2,2]{1,0,5,4,3,2:T(8,128)S(1)}, f32[8,8,2,2,2,2]{1,0,5,4,3,2:T(8,128)}, u32[]{:S(2)}) copy-start(f32[8,8,2,2,2,2]{1,0,5,4,3,2:T(8,128)} %copy.25) | copy-start | bytes 12292
  213.7 67.8 %copy-start.3 = (s32[16]{0:T(128)S(1)}, s32[16]{0:T(128)}, u32[]{:S(2)}) copy-start(s32[16]{0:T(128)} %param.11) | copy-start | bytes 196
  213.7 120.3 %copy-start.1 = (f32[8,8,2,2]{1,3,2,0:T(2,128)S(1)}, f32[8,8,2,2]{1,3,2,0:T(2,128)}, u32[]{:S(2)}) copy-start(f32[8,8,2,2]{1,3,2,0:T(2,128)} %param.8) | copy-start | bytes 3076
  213.7 62.5 %reduce-scatter.7.cloned.1.call-start = ((), (), s32[]{:S(2)}) async-start(), calls=%async_computation.6 | async-start | bytes 1179648
  277.7 9.1 %collective-permute-start = (bf16[128,1536]{1,0:T(8,128)(2,1)S(1)}, bf16[128,1536]{1,0:T(8,128)(2,1)S(1)}, u32[]{:S(2)}, u32[]{:S(2)}) collective-permute-start(bf16[128,1536]{1,0:T(8,128)(2,1)S(1)} %reshape_reshape.3), channel_id=1, source_target_pairs={{8,0},{16,8},{24,16},{32,24},{40,32},{48,40},{56,48},{64,56},{72,6... | collective-permute-start | bytes 1179656 | tf_op jit(solution)/shard_map/ppermute | solution.py:16
  284.2 13.0 %collective-permute-start.2 = (bf16[128,1536]{1,0:T(8,128)(2,1)S(1)}, bf16[128,1536]{1,0:T(8,128)(2,1)S(1)}, u32[]{:S(2)}, u32[]{:S(2)}) collective-permute-start(bf16[128,1536]{1,0:T(8,128)(2,1)S(1)} %reshape_reshape.3), channel_id=1, source_target_pairs={{16,0},{24,8},{32,16},{40,24},{48,32},{56,40},{64,48},{72,56},{80,... | collective-permute-start | bytes 1179656 | tf_op jit(solution)/shard_map/ppermute | solution.py:16
  287.1 9.7 %collective-permute-start.1 = (bf16[128,128]{0,1:T(8,128)(2,1)S(1)}, bf16[128,128]{0,1:T(8,128)(2,1)S(1)}, u32[]{:S(2)}, u32[]{:S(2)}) collective-permute-start(bf16[128,128]{0,1:T(8,128)(2,1)S(1)} %get-tuple-element.12), channel_id=1, source_target_pairs={{0,8},{8,16},{16,24},{24,32},{32,40},{40,48},{48,56},{56,64},{64,7... | collective-permute-start | bytes 98312 | tf_op jit(solution)/shard_map/ppermute | solution.py:16
  295.5 11.1 %collective-permute-start.4 = (bf16[128,1536]{1,0:T(8,128)(2,1)S(1)}, bf16[128,1536]{1,0:T(8,128)(2,1)S(1)}, u32[]{:S(2)}, u32[]{:S(2)}) collective-permute-start(bf16[128,1536]{1,0:T(8,128)(2,1)S(1)} %reshape_reshape.3), channel_id=1, source_target_pairs={{24,0},{32,8},{40,16},{48,24},{56,32},{64,40},{72,48},{80,56},{88,... | collective-permute-start | bytes 1179656 | tf_op jit(solution)/shard_map/ppermute | solution.py:16
  297.4 9.1 %collective-permute-start.3 = (bf16[128,128]{0,1:T(8,128)(2,1)S(1)}, bf16[128,128]{0,1:T(8,128)(2,1)S(1)}, u32[]{:S(2)}, u32[]{:S(2)}) collective-permute-start(bf16[128,128]{0,1:T(8,128)(2,1)S(1)} %get-tuple-element.14), channel_id=1, source_target_pairs={{0,16},{8,24},{16,32},{24,40},{32,48},{40,56},{48,64},{56,72},{64,... | collective-permute-start | bytes 98312 | tf_op jit(solution)/shard_map/ppermute | solution.py:16
  306.9 11.1 %collective-permute-start.5 = (bf16[128,128]{0,1:T(8,128)(2,1)S(1)}, bf16[128,128]{0,1:T(8,128)(2,1)S(1)}, u32[]{:S(2)}, u32[]{:S(2)}) collective-permute-start(bf16[128,128]{0,1:T(8,128)(2,1)S(1)} %get-tuple-element.16), channel_id=1, source_target_pairs={{0,24},{8,32},{16,40},{24,48},{32,56},{40,64},{48,72},{56,80},{64,... | collective-permute-start | bytes 98312 | tf_op jit(solution)/shard_map/ppermute | solution.py:16
  319.0 14.2 %all-to-all-start = ((bf16[8,128,256]{1,2,0:T(8,128)(2,1)}), bf16[8,128,256]{1,2,0:T(8,128)(2,1)S(1)}, u32[]{:S(2)}, u32[]{:S(2)}) async-start(bf16[8,128,256]{1,2,0:T(8,128)(2,1)} %bitcast.20), calls=%async_computation.1 | async-start | bytes 1048576 | tf_op jit(solution)/shard_map/all_to_all | solution.py:32
Sparse Core Ops, SparseCore 0:
  9.7 60.7 all-gather.2
  72.2 102.3 all-gather.4
  213.8 38.5 reduce-scatter.4
  254.9 21.3 reduce-scatter.6
where the time goes:
time: 342 us; the launch traced here: 341 us
  waiting for transfers between devices  195 us (57%)
  local copies, waits for them, and re-layouts  50.6 us (15%)
  matrix products  38.8 us (11%)
  starting transfers between devices  25.3 us (7%)
  between operations  25.3 us (7%)
  other arithmetic  5.29 us (2%)
    all_gather x1, waiting for transfers between devices, shards(): columns_piece = lax.all_gather(right_environment, 'lb', axis=2, tiled=True)  67.1 us
    all_gather x1, waiting for transfers between devices, shards(): rows_piece = lax.all_gather(wavefunction, 'lb', axis=0, tiled=True)  57.6 us
    reduce_scatter x1, waiting for transfers between devices, summed_rows(): value = lax.psum_scatter(value, axis, scatter_dimension=dim, tiled=True)  38.6 us
    all_gather x1, local copies, waits for them, and re-layouts, shards(): columns_piece = lax.all_gather(right_environment, 'lb', axis=2, tiled=True)  24 us
    unnamed x5, waiting for transfers between devices  22.2 us
    ppermute x6, starting transfers between devices, shifted(): return lax.ppermute(value, axis, pairs)  21.2 us
    reshape x1, local copies, waits for them, and re-layouts, shards(): flat_piece = rows_piece.reshape(rows_piece.shape[0], 4 * local_right)  15.5 us
    dot_general x1, matrix products, shards(): jnp.dot(left_matrix, flat_piece, preferred_element_type=jnp.float32)  15.1 us
  transfers between devices with their start and end apart: 11, of which 7 were waited for; matrix products, arithmetic and copies ran while one was open for 15% of the time, Pallas kernels for 0%

commit v1 on v0

--- a/solution.py
+++ b/solution.py
@@ -8,6 +8,11 @@
 BOND_WIDTH = 3072
 SECTOR_TILES = 4
 RB = ("rb_0", "rb_1")
+
+
+def exchange_gather(x, name, dim):
+    sent = jnp.stack([x] * lax.axis_size(name))
+    return jnp.concatenate(lax.all_to_all(sent, name, 0, 0), axis=dim)
 
 
 def shifted(value, axis, by):
@@ -71,7 +76,7 @@
         "avyx,alxr->lyvr", combined, left_part, precision=lax.Precision.HIGHEST
     ).astype(jnp.bfloat16)
     mixed_matrix = mixed_part.reshape(row_count * 4, channels * local_right)
-    columns_piece = lax.all_gather(right_environment, "lb", axis=2, tiled=True)
+    columns_piece = exchange_gather(right_environment, "lb", 2)
     flat_piece = columns_piece.reshape(channels * local_right, columns_piece.shape[2])
     partial_value = jnp.dot(mixed_matrix, flat_piece, preferred_element_type=jnp.float32)
     summed = summed_rows(partial_value.astype(jnp.bfloat16), RB, 1).astype(jnp.float32)

time: 342 us -> 502 us (1.47)
  waiting for transfers between devices: 195 us -> 348 us
  starting transfers between devices: 25.3 us -> 32.7 us
    all_to_all x0 -> x1, waiting for transfers between devices: none -> 276 us  [exchange_gather(): return jnp.concatenate(lax.all_to_all(sent, name, 0, 0), axis=dim)]
    all_gather x1 -> x0, waiting for transfers between devices: 67.1 us -> none  [shards(): columns_piece = lax.all_gather(right_environment, 'lb', axis=2, tiled=True)]
    all_gather x1, waiting for transfers between devices: 57.6 us -> 0.01 us  [shards(): rows_piece = lax.all_gather(wavefunction, 'lb', axis=0, tiled=True)]
    all_gather x1 -> x0, local copies, waits for them, and re-layouts: 24 us -> none  [shards(): columns_piece = lax.all_gather(right_environment, 'lb', axis=2, tiled=True)]
    unnamed x13 -> x16, local copies, waits for them, and re-layouts: 7.98 us -> 25.9 us
    all_to_all x0 -> x1, starting transfers between devices: none -> 7.47 us  [exchange_gather(): return jnp.concatenate(lax.all_to_all(sent, name, 0, 0), axis=dim)]
    another operation x0 -> x1, local copies, waits for them, and re-layouts: none -> 7.04 us  [exchange_gather(): sent = jnp.stack([x] * lax.axis_size(name))]
    unnamed x5 -> x4, waiting for transfers between devices: 22.2 us -> 22.2 us
  transfers between devices with their start and end apart: 11 -> 11, of which waited for: 7 -> 6; matrix products, arithmetic and copies ran while one was open for 15% -> 6% of each run, Pallas kernels for 0% -> 0%
where the time goes in v1:
time: 502 us; the launch traced here: 501 us
  waiting for transfers between devices  348 us (69%)
  local copies, waits for them, and re-layouts  51.4 us (10%)
  matrix products  38.2 us (8%)
  starting transfers between devices  32.7 us (7%)
  between operations  25.3 us (5%)
  other arithmetic  5.29 us (1%)
    all_to_all x1, waiting for transfers between devices, exchange_gather(): return jnp.concatenate(lax.all_to_all(sent, name, 0, 0), axis=dim)  276 us
    reduce_scatter x1, waiting for transfers between devices, summed_rows(): value = lax.psum_scatter(value, axis, scatter_dimension=dim, tiled=True)  40 us
    unnamed x16, local copies, waits for them, and re-layouts  25.9 us
    unnamed x4, waiting for transfers between devices  22.2 us
    ppermute x6, starting transfers between devices, shifted(): return lax.ppermute(value, axis, pairs)  21.2 us
    reshape x1, local copies, waits for them, and re-layouts, shards(): flat_piece = rows_piece.reshape(rows_piece.shape[0], 4 * local_right)  15.4 us
    dot_general x1, matrix products, shards(): jnp.dot(mixed_matrix, flat_piece, preferred_element_type=jnp.float32)  15.3 us
    dot_general x1, matrix products, shards(): jnp.dot(left_matrix, flat_piece, preferred_element_type=jnp.float32)  15 us
  transfers between devices with their start and end apart: 11, of which 6 were waited for; matrix products, arithmetic and copies ran while one was open for 6% of the time, Pallas kernels for 0%

profile of v1, /device:TPU:1, one launch (start us, length us, event | category | flops | bytes accessed | tf_op | source)
XLA Modules:
  0.0 500.8 jit_solution(18230184070983939264)
XLA Ops:
  7.2 2.0 copy.28
  9.1 7.0 %stack.2 = bf16[16,8,384,192]{2,1,3,0:T(8,128)(2,1)} broadcast(bf16[8,384,192]{1,0,2:T(8,128)(2,1)S(1)} %copy.28), dimensions={1,2,3} | broadcast | bytes 20054016 | tf_op jit(solution)/shard_map/stack | solution.py:14
  16.2 7.5 %all-to-all-start = ((bf16[16,8,384,192]{2,1,3,0:T(8,128)(2,1)}), bf16[16,8,384,192]{2,1,3,0:T(8,128)(2,1)}, u32[]{:S(2)}, u32[]{:S(2)}) async-start(bf16[16,8,384,192]{2,1,3,0:T(8,128)(2,1)} %stack.2), calls=%async_computation | async-start | bytes 37748736 | tf_op jit(solution)/shard_map/all_to_all | solution.py:15
  23.7 0.7 all-gather.2.cloned.1.call-update
  24.9 0.7 copy.26
  25.6 275.9 %all-to-all-done = bf16[16,8,384,192]{2,1,3,0:T(8,128)(2,1)} async-done(((bf16[16,8,384,192]{2,1,3,0:T(8,128)(2,1)}), bf16[16,8,384,192]{2,1,3,0:T(8,128)(2,1)}, u32[]{:S(2)}, u32[]{:S(2)}) %all-to-all-start) | async-done | bytes 18874400 | tf_op jit(solution)/shard_map/all_to_all | solution.py:15
  301.5 18.9 %copy.50 = bf16[384,8,8,384]{3,1,2,0:T(8,128)(2,1)} copy(bf16[384,8,8,384]{3,2,1,0:T(8,128)(2,1)} %bitcast.34) | data formatting | bytes 37748736
  320.4 15.4 %copy.41 = bf16[3072,4,384]{0,2,1:T(8,128)(2,1)} copy(bf16[3072,4,384]{2,1,0:T(4,128)(2,1)} %all-gather.2.cloned.1.call-done) | data formatting | bytes 18874368 | tf_op jit(solution)/shard_map/reshape | solution.py:71
  335.8 15.0 %fusion = f32[8,128,4,384]{3,0,2,1:T(8,128)S(1)} fusion(bf16[3072,4,384]{0,2,1:T(8,128)(2,1)} %copy.41, bf16[8,128,3072,1]{2,1,0,3:T(8,128)(2,1)} %bitcast.67), kind=kOutput, calls=%fused_computation | convolution fusion | flops 9663676416 | bytes 22020096 | tf_op jit(solution)/shard_map/dot_general | solution.py:72
  350.9 5.7 %bitcast_convert_fusion = bf16[128,384,8,4]{1,2,3,0:T(8,128)(2,1)S(1)} fusion(f32[8,8,4,4,1]{1,0,3,2,4:T(8,128)S(1)} %bitcast.65, f32[8,128,4,384]{3,0,2,1:T(8,128)S(1)} %fusion), kind=kOutput, calls=%fused_computation.4 | convolution fusion | flops 605552640 | bytes 9441280 | tf_op jit(solution)/shard_map/avyx,alxr->lyvr/dot_general | solution.py:75
  356.5 0.7 copy.49
  357.3 15.3 %convolution_convert_fusion = bf16[512,3072]{1,0:T(8,128)(2,1)} fusion(bf16[512,3072]{1,0:T(8,128)(2,1)S(1)} %bitcast.62, bf16[3072,3072]{0,1:T(8,128)(2,1)} %bitcast.60), kind=kOutput, calls=%fused_computation.6 | convolution fusion | flops 9665249280 | bytes 25165824 | tf_op jit(solution)/shard_map/dot_general | solution.py:81
  372.7 40.0 %reduce-scatter.5.cloned.1.call-done = bf16[512,768]{1,0:T(8,128)(2,1)} async-done(((bf16[512,3072]{1,0:T(8,128)(2,1)}), bf16[512,768]{1,0:T(8,128)(2,1)}) %reduce-scatter.5.cloned.1.call-update) | async-done | bytes 786448 | tf_op jit(solution)/shard_map/reduce_scatter | solution.py:26
  412.7 2.3 copy.47
  415.0 21.5 %reduce-scatter.7.cloned.1.call-done = bf16[384,512]{1,0:T(8,128)(2,1)} async-done(((bf16[768,512]{1,0:T(8,128)(2,1)}), bf16[384,512]{1,0:T(8,128)(2,1)}) %reduce-scatter.7.cloned.1.call-update) | async-done | bytes 393232
  436.5 1.2 copy.48
  437.9 2.6 collective-permute-start
  441.8 0.7 fusion.16
  444.4 1.3 collective-permute-start.2
  445.8 0.9 fusion.7
  447.3 3.4 collective-permute-start.1
  450.7 0.6 compare_reduce_fusion.4
  455.8 1.3 collective-permute-start.4
  457.6 4.1 collective-permute-start.3
  461.8 0.6 compare_reduce_fusion.2
  467.2 8.5 %collective-permute-start.5 = (bf16[128,128]{0,1:T(8,128)(2,1)S(1)}, bf16[128,128]{0,1:T(8,128)(2,1)S(1)}, u32[]{:S(2)}, u32[]{:S(2)}) collective-permute-start(bf16[128,128]{0,1:T(8,128)(2,1)S(1)} %get-tuple-element.16), channel_id=1, source_target_pairs={{0,24},{8,32},{16,40},{24,48},{32,56},{40,64},{48,72},{56,80},{64,... | collective-permute-start | bytes 98312 | tf_op jit(solution)/shard_map/ppermute | solution.py:21
  475.7 0.6 compare_reduce_fusion
  478.4 0.8 slice.7
  479.3 4.0 all-to-all-start.1
  483.2 0.8 reshape.33
  484.1 9.3 %all-to-all-done.1 = bf16[8,128,256]{1,2,0:T(8,128)(2,1)S(1)} async-done(((bf16[8,128,256]{1,2,0:T(8,128)(2,1)}), bf16[8,128,256]{1,2,0:T(8,128)(2,1)S(1)}, u32[]{:S(2)}, u32[]{:S(2)}) %all-to-all-start.1) | async-done | bytes 524320 | tf_op jit(solution)/shard_map/all_to_all | solution.py:37
  493.5 0.8 copy.32
  (43 shorter events, 5.3 us)
Async XLA Ops:
  7.2 17.3 %copy-start = (f32[8,8,2,2]{1,3,2,0:T(2,128)S(1)}, f32[8,8,2,2]{1,3,2,0:T(2,128)}, u32[]{:S(2)}) copy-start(f32[8,8,2,2]{1,3,2,0:T(2,128)} %param.8) | copy-start | bytes 3076
  16.2 8.3 %copy-start.3 = (f32[8,8,2,2]{1,3,2,0:T(2,128)S(1)}, f32[8,8,2,2]{1,3,2,0:T(2,128)}, u32[]{:S(2)}) copy-start(f32[8,8,2,2]{1,3,2,0:T(2,128)} %param.9) | copy-start | bytes 3076
  16.2 285.3 %all-to-all-start = ((bf16[16,8,384,192]{2,1,3,0:T(8,128)(2,1)}), bf16[16,8,384,192]{2,1,3,0:T(8,128)(2,1)}, u32[]{:S(2)}, u32[]{:S(2)}) async-start(bf16[16,8,384,192]{2,1,3,0:T(8,128)(2,1)} %stack.2), calls=%async_computation | async-start | bytes 37748736 | tf_op jit(solution)/shard_map/all_to_all | solution.py:15
  23.7 296.7 %all-gather.2.cloned.1.call-start = ((), (), s32[]{:S(2)}) async-start(), calls=%async_computation.4 | async-start | bytes 10027008 | tf_op jit(solution)/shard_map/all_gather | solution.py:70
  24.4 388.3 %reduce-scatter.5.cloned.1.call-start = ((), (), s32[]{:S(2)}) async-start(), calls=%async_computation.5 | async-start | bytes 3932160 | tf_op jit(solution)/shard_map/reduce_scatter | solution.py:26
  335.8 15.0 %copy-start.2 = (f32[8,8,2,2,2,2]{1,0,5,4,3,2:T(8,128)S(1)}, f32[8,8,2,2,2,2]{1,0,5,4,3,2:T(8,128)}, u32[]{:S(2)}) copy-start(f32[8,8,2,2,2,2]{1,0,5,4,3,2:T(8,128)} %copy.26) | copy-start | bytes 12292
  372.6 69.2 %copy-start.4 = (s32[16]{0:T(128)S(1)}, s32[16]{0:T(128)}, u32[]{:S(2)}) copy-start(s32[16]{0:T(128)} %param.11) | copy-start | bytes 196
  372.6 121.6 %copy-start.1 = (f32[8,8,2,2]{1,3,2,0:T(2,128)S(1)}, f32[8,8,2,2]{1,3,2,0:T(2,128)}, u32[]{:S(2)}) copy-start(f32[8,8,2,2]{1,3,2,0:T(2,128)} %param.8) | copy-start | bytes 3076
  372.6 63.8 %reduce-scatter.7.cloned.1.call-start = ((), (), s32[]{:S(2)}) async-start(), calls=%async_computation.6 | async-start | bytes 1179648
  437.9 9.1 %collective-permute-start = (bf16[128,1536]{1,0:T(8,128)(2,1)S(1)}, bf16[128,1536]{1,0:T(8,128)(2,1)S(1)}, u32[]{:S(2)}, u32[]{:S(2)}) collective-permute-start(bf16[128,1536]{1,0:T(8,128)(2,1)S(1)} %reshape_reshape.7), channel_id=1, source_target_pairs={{8,0},{16,8},{24,16},{32,24},{40,32},{48,40},{56,48},{64,56},{72,6... | collective-permute-start | bytes 1179656 | tf_op jit(solution)/shard_map/ppermute | solution.py:21
  444.4 13.0 %collective-permute-start.2 = (bf16[128,1536]{1,0:T(8,128)(2,1)S(1)}, bf16[128,1536]{1,0:T(8,128)(2,1)S(1)}, u32[]{:S(2)}, u32[]{:S(2)}) collective-permute-start(bf16[128,1536]{1,0:T(8,128)(2,1)S(1)} %reshape_reshape.7), channel_id=1, source_target_pairs={{16,0},{24,8},{32,16},{40,24},{48,32},{56,40},{64,48},{72,56},{80,... | collective-permute-start | bytes 1179656 | tf_op jit(solution)/shard_map/ppermute | solution.py:21
  447.3 9.7 %collective-permute-start.1 = (bf16[128,128]{0,1:T(8,128)(2,1)S(1)}, bf16[128,128]{0,1:T(8,128)(2,1)S(1)}, u32[]{:S(2)}, u32[]{:S(2)}) collective-permute-start(bf16[128,128]{0,1:T(8,128)(2,1)S(1)} %get-tuple-element.12), channel_id=1, source_target_pairs={{0,8},{8,16},{16,24},{24,32},{32,40},{40,48},{48,56},{56,64},{64,7... | collective-permute-start | bytes 98312 | tf_op jit(solution)/shard_map/ppermute | solution.py:21
  455.8 11.1 %collective-permute-start.4 = (bf16[128,1536]{1,0:T(8,128)(2,1)S(1)}, bf16[128,1536]{1,0:T(8,128)(2,1)S(1)}, u32[]{:S(2)}, u32[]{:S(2)}) collective-permute-start(bf16[128,1536]{1,0:T(8,128)(2,1)S(1)} %reshape_reshape.7), channel_id=1, source_target_pairs={{24,0},{32,8},{40,16},{48,24},{56,32},{64,40},{72,48},{80,56},{88,... | collective-permute-start | bytes 1179656 | tf_op jit(solution)/shard_map/ppermute | solution.py:21
  457.6 9.1 %collective-permute-start.3 = (bf16[128,128]{0,1:T(8,128)(2,1)S(1)}, bf16[128,128]{0,1:T(8,128)(2,1)S(1)}, u32[]{:S(2)}, u32[]{:S(2)}) collective-permute-start(bf16[128,128]{0,1:T(8,128)(2,1)S(1)} %get-tuple-element.14), channel_id=1, source_target_pairs={{0,16},{8,24},{16,32},{24,40},{32,48},{40,56},{48,64},{56,72},{64,... | collective-permute-start | bytes 98312 | tf_op jit(solution)/shard_map/ppermute | solution.py:21
  467.2 11.1 %collective-permute-start.5 = (bf16[128,128]{0,1:T(8,128)(2,1)S(1)}, bf16[128,128]{0,1:T(8,128)(2,1)S(1)}, u32[]{:S(2)}, u32[]{:S(2)}) collective-permute-start(bf16[128,128]{0,1:T(8,128)(2,1)S(1)} %get-tuple-element.16), channel_id=1, source_target_pairs={{0,24},{8,32},{16,40},{24,48},{32,56},{40,64},{48,72},{56,80},{64,... | collective-permute-start | bytes 98312 | tf_op jit(solution)/shard_map/ppermute | solution.py:21
  479.3 14.2 %all-to-all-start.1 = ((bf16[8,128,256]{1,2,0:T(8,128)(2,1)}), bf16[8,128,256]{1,2,0:T(8,128)(2,1)S(1)}, u32[]{:S(2)}, u32[]{:S(2)}) async-start(bf16[8,128,256]{1,2,0:T(8,128)(2,1)} %bitcast.20), calls=%async_computation.2 | async-start | bytes 1048576 | tf_op jit(solution)/shard_map/all_to_all | solution.py:37
Sparse Core Ops, SparseCore 0:
  26.2 244.9 all-gather.1
  372.8 39.8 reduce-scatter.4
  415.1 21.3 reduce-scatter.6
